TPU v7x, 256 devices: a whole 4x4x8 slice. The times are simulated.
256 devices in a mesh: blk: 32 (over z, x_hi, core), rel: 8 (over x_lo, y).
Axes of the slice: x: 4 (x_hi: 2, x_lo: 2; x = x_hi * 2 + x_lo), y: 4, z: 8, core: 2. Of those that a mesh axis runs over, the one named last changes fastest.
Arguments:
- left_slab: float32 [524288, 400], P(('blk', 'rel')), may hold values from -1.3 to 1.3
- left_state: float32 [524288], P(('blk', 'rel')), may hold values from 1e-05 to 0.0001
- right_slab: float32 [524288, 400], P(('blk', 'rel')), may hold values from -1.3 to 1.3
- right_state: float32 [524288], P(('blk', 'rel')), may hold values from 1e-05 to 0.0001
- relations: float32 [32, 400], replicated, may hold values from 0.1 to 1.9
- relation_state: float32 [32], replicated, may hold values from 0.01 to 0.2
- src_index: int32 [2, 65536], P(None, ('blk', 'rel')), may hold values from 0 to 2047
- dst_index: int32 [2, 65536], P(None, ('blk', 'rel')), may hold values from 0 to 2047
- relation_id: int32 [2, 65536], P(None, ('blk', 'rel')), may hold values from 0 to 31
- neg_source: int32 [2, 256000], P(None, ('blk', 'rel')), may hold values from 0 to 2047
- neg_target: int32 [2, 256000], P(None, ('blk', 'rel')), may hold values from 0 to 2047
Outputs:
- left_out: float32 [524288, 400], P(('blk', 'rel'))
- right_out: float32 [524288, 400], P(('blk', 'rel'))
- relations_out: float32 [32, 32, 400], P('blk')
All inputs are finite; a program needn't handle non-finite values.
Results may differ from a plain program's by a relative error of at most 0.00069.
Values sent between devices are 32-bit elements; how exact they have to be, the bound alone decides.
A program may use at most 64 MiB of HBM per device.

v0:
```python
import jax
import jax.numpy as jnp
from jax import lax
from jax.experimental import pallas as pl
from jax.experimental.pallas import tpu as pltpu
from jax.sharding import PartitionSpec as P

rate = 0.1
D = 400
ROWS = 2048
EDGES = 256
NEG = 1000
NREL = 32
CHUNK = 256
CHUNKS = ROWS // CHUNK
PIECES = 5
FLIGHT = 3
LATER = {2: 5, 7: 6}
MESH = pl.DeviceIdType.MESH
f32 = jnp.float32
bf16 = jnp.bfloat16


def iota(shape, axis):
    return lax.broadcasted_iota(jnp.int32, shape, axis)


def dot(a, b, ca, cb, precision=None):
    return lax.dot_general(
        a, b, (((ca,), (cb,)), ((), ())), precision=precision, preferred_element_type=f32
    )


def halves(x):
    high = x.astype(bf16)
    return high, (x - high.astype(f32)).astype(bf16)


def cut(c):
    return slice(c * CHUNK, (c + 1) * CHUNK)


def hot_chunk(index_row, c):
    return jnp.where(iota((CHUNK, EDGES), 0) + c * CHUNK == index_row, 1.0, 0.0).astype(bf16)


def count_rows(index_row):
    high = index_row // 128
    low = index_row - 128 * high
    hot_high = jnp.where(iota((16, 1024), 0) == high, 1.0, 0.0).astype(bf16)
    hot_low = jnp.where(iota((128, 1024), 0) == low, 1.0, 0.0).astype(bf16)
    return dot(hot_high, hot_low, 1, 1)


def kernel(
    left,
    lstate,
    right,
    rstate,
    relations,
    relation_state,
    src,
    dst,
    rid,
    nsrc,
    ndst,
    left_m,
    main1,
    rel_all,
    rel_old,
    rel_state,
    left_b,
    left_s,
    right_b,
    main0,
    state0,
    state1,
    drawn,
    often_l,
    often_r,
    hot_src,
    hot_dst,
    source,
    target,
    weight,
    query,
    query_t,
    probe,
    probe_t,
    gq,
    gp,
    grad_l,
    grad_r,
    rel_sum,
    local_sem,
    send_sem,
    recv_sem,
    rsend_sem,
    rrecv_sem,
):

    blk, rel = lax.axis_index("blk"), lax.axis_index("rel")
    blks, rels = lax.axis_size("blk"), lax.axis_size("rel")
    after = (lax.rem(blk + 1, blks), rel)
    before = (lax.rem(blk + blks - 1, blks), rel)
    core = lax.rem(blk, 2)

    get_left = pltpu.make_async_copy(left, left_m, local_sem.at[0])
    get_left.start()

    barrier = pltpu.get_barrier_semaphore()
    pl.semaphore_signal(barrier, inc=1, device_id=before, device_id_type=MESH)
    for k in range(1, rels):
        peer = (blk, lax.rem(rel + k, rels))
        pl.semaphore_signal(barrier, inc=1, device_id=peer, device_id_type=MESH)
    pl.semaphore_wait(barrier, rels)

    def send(src_ref, dst_ref, t, i):
        return pltpu.make_async_remote_copy(
            src_ref=src_ref,
            dst_ref=dst_ref,
            send_sem=send_sem.at[t, i],
            recv_sem=recv_sem.at[t, i],
            device_id=after,
            device_id_type=MESH,
        )

    mains, states = (main0, main1), (state0, state1)
    moves = (
        [send(right.at[:, cut(c)], main0.at[:, cut(c)], 0, c) for c in range(CHUNKS)]
        + [send(rstate, state0, 0, CHUNKS)],
        [send(main0.at[:, cut(c)], main1.at[:, cut(c)], 1, c) for c in range(CHUNKS)]
        + [send(state0, state1, 1, CHUNKS)],
    )
    for move in moves[0]:
        move.start()

    rel_old[...] = relations[...]
    own = jnp.broadcast_to(relation_state[...], (NREL, NREL))
    diagonal = iota((NREL, NREL), 0) == iota((NREL, NREL), 1)
    own = jnp.sum(jnp.where(diagonal, own, 0.0), axis=1, keepdims=True)
    rel_state[...] = jnp.broadcast_to(own, (NREL, 128))
    left_s[...] = lstate[...]
    get_left.wait()

    def left_side(t):
        drawn[...] = jnp.full(drawn.shape, -1, jnp.int32)
        drawn[0:1, 0:NEG] = nsrc[t : t + 1, :]
        drawn[1:2, 0:NEG] = ndst[t : t + 1, :]
        often_l[...] = count_rows(drawn[0:1, :])
        often_r[...] = count_rows(drawn[1:2, :])
        hot_rel = jnp.where(iota((NREL, EDGES), 0) == rid[t : t + 1, :], 1.0, 0.0)
        weight[...] = dot(relations[...], hot_rel, 0, 0, lax.Precision.HIGHEST)
        source[...] = jnp.zeros_like(source)
        for c in range(CHUNKS):
            hot_src[cut(c), :] = hot_chunk(src[t : t + 1, :], c)
            hot_dst[cut(c), :] = hot_chunk(dst[t : t + 1, :], c)
            pick(left_m, left_b, hot_src, source, c)
        q = source[...] * weight[...]
        query_t[...] = q.astype(bf16)
        query[...] = q.T.astype(bf16)

    def pick(main, rounded, hot, out, c):
        x = main[:, cut(c)]
        high = x.astype(bf16)
        rest = x - high.astype(f32)
        middle, low = halves(rest)
        rounded[:, cut(c)] = high
        table = hot[cut(c), :]
        out[...] += dot(high, table, 1, 0) + (dot(middle, table, 1, 0) + dot(low, table, 1, 0))

    def negatives(mine, mine_t, slab, often, sum_ref, grad_ref, c):
        rows = slab[:, cut(c)]
        score = dot(mine[...], rows, 1, 0)
        g = ((0.5 * jnp.tanh(0.5 * score) + 0.5) / NEG).astype(bf16)
        times = jnp.concatenate([often[2 * c : 2 * c + 1, :], often[2 * c + 1 : 2 * c + 2, :]], axis=1)
        sum_ref[...] += dot(rows, (g.astype(f32) * times).astype(bf16), 1, 1)
        grad_ref[:, cut(c)] = dot(mine_t[...], g, 1, 0) * times

    def feed(c):
        @pl.when(core == 1)
        def _():
            moves[1][c - FLIGHT].wait_send()
            moves[1][c].start()

    def gradients(t):
        target[...] = jnp.zeros_like(target)
        gq[...] = jnp.zeros_like(gq)
        gp[...] = jnp.zeros_like(gp)
        moves[t][CHUNKS].wait_recv()
        for c in range(CHUNKS):
            moves[t][c].wait_recv()
            pick(mains[t], right_b, hot_dst, target, c)
            negatives(query, query_t, right_b, often_r, gq, grad_r, c)
            if t == 1 and c in LATER:
                feed(LATER[c])
        p = weight[...] * target[...]
        probe_t[...] = p.astype(bf16)
        probe[...] = p.T.astype(bf16)
        for c in range(CHUNKS):
            negatives(probe, probe_t, left_b, often_l, gp, grad_l, c)
        if t == 1:
            feed(7)
        s, w, y = source[...], weight[...], target[...]
        pos = jnp.sum(s * w * y, axis=0, keepdims=True)
        coef = -1.0 / (1.0 + jnp.exp(pos))
        q, p = gq[...], gp[...]
        g_weight = coef * s * y + q * s + p * y
        hot_rel = jnp.where(iota((NREL, EDGES), 0) == rid[t : t + 1, :], 1.0, 0.0)
        g_rel = dot(hot_rel, g_weight, 1, 1, lax.Precision.HIGHEST)
        return coef * w * y + q * w, coef * w * s + p * w, g_rel

    def update(c, high, low, hot, grad_ref, main, state):
        table = hot[cut(c), :]
        grad = grad_ref[:, cut(c)] + (dot(high, table, 1, 1) + dot(low, table, 1, 1))
        new_state = state[:, cut(c)] + jnp.sum(grad * grad, axis=0, keepdims=True) / D
        state[:, cut(c)] = new_state
        main[:, cut(c)] = main[:, cut(c)] - grad * (rate / jnp.sqrt(new_state))

    left_side(0)
    g_source, g_target, g_rel = gradients(0)
    rel_sum[...] = g_rel
    high, low = halves(g_target)
    for c in range(CHUNKS):
        update(c, high, low, hot_dst, grad_r, main0, state0)
        if c < FLIGHT:
            moves[1][c].start()
        else:

            @pl.when(core == 0)
            def _():
                moves[1][c].start()

    moves[1][CHUNKS].start()
    high, low = halves(g_source)
    for c in range(CHUNKS):
        update(c, high, low, hot_src, grad_l, left_m, left_s)

    left_side(1)
    feed(3)
    feed(4)
    g_source, g_target, g_rel = gradients(1)
    rel_sum[...] += g_rel
    rel_all[rel] = rel_sum[...]
    shares = []
    for k in range(1, rels):
        shares.append(
            pltpu.make_async_remote_copy(
                src_ref=rel_sum,
                dst_ref=rel_all.at[rel],
                send_sem=rsend_sem.at[k],
                recv_sem=rrecv_sem.at[k],
                device_id=(blk, lax.rem(rel + k, rels)),
                device_id_type=MESH,
            )
        )
        shares[-1].start()

    high, low = halves(g_target)
    for c in range(CHUNKS):
        update(c, high, low, hot_dst, grad_r, main1, state1)

    high, low = halves(g_source)
    for c in range(CHUNKS):
        update(c, high, low, hot_src, grad_l, left_m, left_s)

    for move in moves[0] + moves[1][CHUNKS - FLIGHT :]:
        move.wait_send()

    @pl.when(core == 0)
    def _():
        for move in moves[1][: CHUNKS - FLIGHT]:
            move.wait_send()

    for copy in shares:
        copy.wait()


def put_out(
    left, right, rel_all, rel_old, rel_state, left_out, right_out, relations_out, sem
):
    puts = []
    for c in range(PIECES):
        rows = slice(c * (D // PIECES), (c + 1) * (D // PIECES))
        puts.append(pltpu.make_async_copy(left.at[rows, :], left_out.at[rows, :], sem.at[2 * c]))
        puts.append(pltpu.make_async_copy(right.at[rows, :], right_out.at[rows, :], sem.at[2 * c + 1]))
    for put in puts:
        put.start()
    total = rel_all[0]
    for k in range(1, rel_all.shape[0]):
        total = total + rel_all[k]
    state = rel_state[:, 0:1] + jnp.sum(total * total, axis=1, keepdims=True) / D
    relations_out[0, :, :] = rel_old[...] - rate * total / jnp.sqrt(state)
    for put in puts:
        put.wait()


def local(
    left_slab,
    left_state,
    right_slab,
    right_state,
    relations,
    relation_state,
    src_index,
    dst_index,
    relation_id,
    neg_source,
    neg_target,
):
    vmem = pl.BlockSpec(memory_space=pltpu.VMEM)
    hbm = pl.BlockSpec(memory_space=pltpu.HBM)
    rels = lax.axis_size("rel")
    slab = pltpu.VMEM((D, ROWS), f32)
    rounded = pltpu.VMEM((D, ROWS), bf16)
    row = pltpu.VMEM((1, ROWS), f32)
    hot = pltpu.VMEM((ROWS, EDGES), bf16)
    edge = pltpu.VMEM((D, EDGES), f32)
    pin = pltpu.with_memory_space_constraint
    given = (
        left_slab.T,
        left_state.reshape(1, ROWS),
        right_slab.T,
        right_state.reshape(1, ROWS),
        relations,
        relation_state.reshape(1, NREL),
        src_index,
        dst_index,
        relation_id,
        neg_source,
        neg_target,
    )
    held = pl.pallas_call(
        kernel,
        out_shape=(
            pltpu.VMEM((D, ROWS), f32),
            pltpu.VMEM((D, ROWS), f32),
            pltpu.VMEM((rels, NREL, D), f32),
            pltpu.VMEM((NREL, D), f32),
            pltpu.VMEM((NREL, 128), f32),
        ),
        in_specs=[hbm, vmem, hbm] + [vmem] * 8,
        out_specs=(vmem,) * 5,
        scratch_shapes=[
            rounded,
            row,
            rounded,
            slab,
            row,
            row,
            pltpu.VMEM((8, 1024), jnp.int32),
            pltpu.VMEM((16, 128), f32),
            pltpu.VMEM((16, 128), f32),
            hot,
            hot,
            edge,
            edge,
            edge,
            pltpu.VMEM((EDGES, D), bf16),
            pltpu.VMEM((D, EDGES), bf16),
            pltpu.VMEM((EDGES, D), bf16),
            pltpu.VMEM((D, EDGES), bf16),
            edge,
            edge,
            slab,
            slab,
            pltpu.VMEM((NREL, D), f32),
            pltpu.SemaphoreType.DMA((1,)),
            pltpu.SemaphoreType.DMA((2, CHUNKS + 1)),
            pltpu.SemaphoreType.DMA((2, CHUNKS + 1)),
            pltpu.SemaphoreType.DMA((rels,)),
            pltpu.SemaphoreType.DMA((rels,)),
        ],
        compiler_params=pltpu.CompilerParams(
            collective_id=0, has_side_effects=True, vmem_limit_bytes=40 * 2**20
        ),
        name="train",
    )(*[pin(x, pltpu.HBM) for x in given])
    left, right, relations_out = pl.pallas_call(
        put_out,
        out_shape=(
            jax.ShapeDtypeStruct((D, ROWS), f32),
            jax.ShapeDtypeStruct((D, ROWS), f32),
            jax.ShapeDtypeStruct((1, NREL, D), f32),
        ),
        in_specs=[vmem, vmem, vmem, vmem, vmem],
        out_specs=(hbm, hbm, vmem),
        scratch_shapes=[pltpu.SemaphoreType.DMA((2 * PIECES,))],
        compiler_params=pltpu.CompilerParams(vmem_limit_bytes=4 * 2**20),
        name="put_out",
    )(*[pin(x, pltpu.VMEM) for x in held])
    return left.T, right.T, relations_out


def solution(mesh):
    in_specs = (
        P(("blk", "rel"), None),
        P(("blk", "rel")),
        P(("blk", "rel"), None),
        P(("blk", "rel")),
        P(),
        P(),
        P(None, ("blk", "rel")),
        P(None, ("blk", "rel")),
        P(None, ("blk", "rel")),
        P(None, ("blk", "rel")),
        P(None, ("blk", "rel")),
    )
    out_specs = (P(("blk", "rel"), None), P(("blk", "rel"), None), P("blk", None, None))
    return jax.shard_map(local, mesh=mesh, in_specs=in_specs, out_specs=out_specs, check_vma=False)
```

profile of v0, /device:TPU:26, one launch (start us, length us, event | category | flops | bytes accessed | tf_op | source)
XLA Modules:
  0.0 99.2 jit_solution(9582442712920667201)
XLA Ops:
  0.6 95.0 %train.1 = (f32[400,2048]{1,0:T(8,128)S(1)}, f32[400,2048]{1,0:T(8,128)S(1)}, f32[8,32,400]{2,1,0:T(8,128)S(1)}, f32[32,400]{1,0:T(8,128)S(1)}, f32[32,128]{1,0:T(8,128)S(1)}) custom-call(f32[400,2048]{1,0:T(8,128)} %bitcast.7, f32[1,2048]{1,0:T(1,128)} %bitcast.9, f32[400,2048]{1,0:T(8,128)} %bitcast.8, f32[1,2048]{1,0:T(1,128)} %bitcast.10, ...), custom_call_target="tpu_custom_call" | custom-call | tf_op jit(solution)/shard_map/train/pallas_call | solution.py:333
  95.6 3.5 %put_out.1 = (f32[400,2048]{1,0:T(8,128)}, f32[400,2048]{1,0:T(8,128)}, f32[1,32,400]{2,1,0:T(8,128)}) custom-call(f32[400,2048]{1,0:T(8,128)S(1)} %get-tuple-element.11.left, f32[400,2048]{1,0:T(8,128)S(1)} %get-tuple-element.12.right, f32[8,32,400]{2,1,0:T(8,128)S(1)} %get-tuple-element.13.rel_all, f32[32,400]{1,0:T(8,128)S(1)} %get-tuple-element.14.rel_old, ...), custom_call_target="tpu_custom_call" | custom-call | tf_op jit(solution)/shard_map/put_out/pallas_call | solution.py:379
where the time goes:
time: 99.4 us; the launch traced here: 99.2 us
  Pallas kernels  98.4 us (99%)
    pallas_call x1, Pallas kernels, local(): pl.pallas_call(kernel, out_shape=(pltpu.VMEM((D, ROWS), f32), pltpu.VMEM(...  95 us
    pallas_call x1, Pallas kernels, local(): pl.pallas_call(put_out, out_shape=(jax.ShapeDtypeStruct((D, ROWS), f32),...  3.48 us

commit v1 on v0

--- a/solution.py
+++ b/solution.py
@@ -13,9 +13,9 @@
 NREL = 32
 CHUNK = 256
 CHUNKS = ROWS // CHUNK
-PIECES = 5
+PIECES = 2
 FLIGHT = 3
-LATER = {2: 5, 7: 6}
+LATER = {2: 6, 7: 7}
 MESH = pl.DeviceIdType.MESH
 f32 = jnp.float32
 bf16 = jnp.bfloat16
@@ -59,16 +59,22 @@
     rstate,
     relations,
     relation_state,
+    src_in,
+    dst_in,
+    rid_in,
+    nsrc_in,
+    ndst_in,
+    left_m,
+    main1,
+    rel_all,
+    rel_old,
+    rel_state,
+    rel_row,
     src,
     dst,
     rid,
     nsrc,
     ndst,
-    left_m,
-    main1,
-    rel_all,
-    rel_old,
-    rel_state,
     left_b,
     left_s,
     right_b,
@@ -89,9 +95,10 @@
     probe_t,
     gq,
     gp,
-    grad_l,
+    g_left,
     grad_r,
     rel_sum,
+    rel_pair,
     local_sem,
     send_sem,
     recv_sem,
@@ -105,14 +112,25 @@
     before = (lax.rem(blk + blks - 1, blks), rel)
     core = lax.rem(blk, 2)
 
-    get_left = pltpu.make_async_copy(left, left_m, local_sem.at[0])
-    get_left.start()
-
     barrier = pltpu.get_barrier_semaphore()
     pl.semaphore_signal(barrier, inc=1, device_id=before, device_id_type=MESH)
     for k in range(1, rels):
         peer = (blk, lax.rem(rel + k, rels))
         pl.semaphore_signal(barrier, inc=1, device_id=peer, device_id_type=MESH)
+    pairs = (
+        (src_in, src),
+        (dst_in, dst),
+        (rid_in, rid),
+        (nsrc_in, nsrc),
+        (ndst_in, ndst),
+        (relations, rel_old),
+        (relation_state, rel_row),
+        (lstate, left_s),
+        (left, left_m),
+    )
+    gets = [pltpu.make_async_copy(a, b, local_sem.at[i]) for i, (a, b) in enumerate(pairs)]
+    for get in gets:
+        get.start()
     pl.semaphore_wait(barrier, rels)
 
     def send(src_ref, dst_ref, t, i):
@@ -135,13 +153,12 @@
     for move in moves[0]:
         move.start()
 
-    rel_old[...] = relations[...]
-    own = jnp.broadcast_to(relation_state[...], (NREL, NREL))
+    for get in gets:
+        get.wait()
+    own = jnp.broadcast_to(rel_row[...], (NREL, NREL))
     diagonal = iota((NREL, NREL), 0) == iota((NREL, NREL), 1)
     own = jnp.sum(jnp.where(diagonal, own, 0.0), axis=1, keepdims=True)
     rel_state[...] = jnp.broadcast_to(own, (NREL, 128))
-    left_s[...] = lstate[...]
-    get_left.wait()
 
     def left_side(t):
         drawn[...] = jnp.full(drawn.shape, -1, jnp.int32)
@@ -150,7 +167,7 @@
         often_l[...] = count_rows(drawn[0:1, :])
         often_r[...] = count_rows(drawn[1:2, :])
         hot_rel = jnp.where(iota((NREL, EDGES), 0) == rid[t : t + 1, :], 1.0, 0.0)
-        weight[...] = dot(relations[...], hot_rel, 0, 0, lax.Precision.HIGHEST)
+        weight[...] = dot(rel_old[...], hot_rel, 0, 0, lax.Precision.HIGHEST)
         source[...] = jnp.zeros_like(source)
         for c in range(CHUNKS):
             hot_src[cut(c), :] = hot_chunk(src[t : t + 1, :], c)
@@ -158,7 +175,7 @@
             pick(left_m, left_b, hot_src, source, c)
         q = source[...] * weight[...]
         query_t[...] = q.astype(bf16)
-        query[...] = q.T.astype(bf16)
+        query[...] = q.T.astype(bf16) * 0.5
 
     def pick(main, rounded, hot, out, c):
         x = main[:, cut(c)]
@@ -169,13 +186,12 @@
         table = hot[cut(c), :]
         out[...] += dot(high, table, 1, 0) + (dot(middle, table, 1, 0) + dot(low, table, 1, 0))
 
-    def negatives(mine, mine_t, slab, often, sum_ref, grad_ref, c):
-        rows = slab[:, cut(c)]
-        score = dot(mine[...], rows, 1, 0)
-        g = ((0.5 * jnp.tanh(0.5 * score) + 0.5) / NEG).astype(bf16)
-        times = jnp.concatenate([often[2 * c : 2 * c + 1, :], often[2 * c + 1 : 2 * c + 2, :]], axis=1)
-        sum_ref[...] += dot(rows, (g.astype(f32) * times).astype(bf16), 1, 1)
-        grad_ref[:, cut(c)] = dot(mine_t[...], g, 1, 0) * times
+    def times(often, c):
+        return jnp.concatenate([often[2 * c : 2 * c + 1, :], often[2 * c + 1 : 2 * c + 2, :]], axis=1)
+
+    def slope(mine, rows):
+        half_score = dot(mine[...], rows, 1, 0)
+        return (jnp.tanh(half_score) * (0.5 / NEG) + 0.5 / NEG).astype(bf16)
 
     def feed(c):
         @pl.when(core == 1)
@@ -183,7 +199,7 @@
             moves[1][c - FLIGHT].wait_send()
             moves[1][c].start()
 
-    def gradients(t):
+    def gradients(t, share):
         target[...] = jnp.zeros_like(target)
         gq[...] = jnp.zeros_like(gq)
         gp[...] = jnp.zeros_like(gp)
@@ -191,38 +207,50 @@
         for c in range(CHUNKS):
             moves[t][c].wait_recv()
             pick(mains[t], right_b, hot_dst, target, c)
-            negatives(query, query_t, right_b, often_r, gq, grad_r, c)
+            rows = right_b[:, cut(c)]
+            g = slope(query, rows)
+            gq[...] += dot(rows, (g.astype(f32) * times(often_r, c)).astype(bf16), 1, 1)
+            grad_r[:, cut(c)] = dot(query_t[...], g, 1, 0) * times(often_r, c)
             if t == 1 and c in LATER:
                 feed(LATER[c])
         p = weight[...] * target[...]
         probe_t[...] = p.astype(bf16)
-        probe[...] = p.T.astype(bf16)
-        for c in range(CHUNKS):
-            negatives(probe, probe_t, left_b, often_l, gp, grad_l, c)
-        if t == 1:
-            feed(7)
+        probe[...] = p.T.astype(bf16) * 0.5
+        for c in range(0, CHUNKS, 2):
+            both = slice(c * CHUNK, (c + 2) * CHUNK)
+            rows = left_b[:, both]
+            g = slope(probe, rows)
+            g_left[:, both] = g
+            often = jnp.concatenate([times(often_l, c), times(often_l, c + 1)], axis=1)
+            gp[...] += dot(rows, (g.astype(f32) * often).astype(bf16), 1, 1)
         s, w, y = source[...], weight[...], target[...]
         pos = jnp.sum(s * w * y, axis=0, keepdims=True)
         coef = -1.0 / (1.0 + jnp.exp(pos))
         q, p = gq[...], gp[...]
         g_weight = coef * s * y + q * s + p * y
-        hot_rel = jnp.where(iota((NREL, EDGES), 0) == rid[t : t + 1, :], 1.0, 0.0)
-        g_rel = dot(hot_rel, g_weight, 1, 1, lax.Precision.HIGHEST)
-        return coef * w * y + q * w, coef * w * s + p * w, g_rel
-
-    def update(c, high, low, hot, grad_ref, main, state):
+        hot_rel = jnp.where(iota((NREL, EDGES), 0) == rid[t : t + 1, :], 1.0, 0.0).astype(bf16)
+        high, low = halves(g_weight)
+        share(dot(hot_rel, high, 1, 1) + dot(hot_rel, low, 1, 1))
+        return coef * w * y + q * w, coef * w * s + p * w
+
+    def update(c, high, low, hot, drawn_grad, main, state):
         table = hot[cut(c), :]
-        grad = grad_ref[:, cut(c)] + (dot(high, table, 1, 1) + dot(low, table, 1, 1))
+        grad = drawn_grad + (dot(high, table, 1, 1) + dot(low, table, 1, 1))
         new_state = state[:, cut(c)] + jnp.sum(grad * grad, axis=0, keepdims=True) / D
         state[:, cut(c)] = new_state
         main[:, cut(c)] = main[:, cut(c)] - grad * (rate / jnp.sqrt(new_state))
 
+    def left_grad(c):
+        return dot(probe_t[...], g_left[:, cut(c)], 1, 0) * times(often_l, c)
+
+    def keep(g_rel):
+        rel_sum[...] = g_rel
+
     left_side(0)
-    g_source, g_target, g_rel = gradients(0)
-    rel_sum[...] = g_rel
+    g_source, g_target = gradients(0, keep)
     high, low = halves(g_target)
     for c in range(CHUNKS):
-        update(c, high, low, hot_dst, grad_r, main0, state0)
+        update(c, high, low, hot_dst, grad_r[:, cut(c)], main0, state0)
         if c < FLIGHT:
             moves[1][c].start()
         else:
@@ -234,35 +262,66 @@
     moves[1][CHUNKS].start()
     high, low = halves(g_source)
     for c in range(CHUNKS):
-        update(c, high, low, hot_src, grad_l, left_m, left_s)
+        update(c, high, low, hot_src, left_grad(c), left_m, left_s)
 
     left_side(1)
     feed(3)
     feed(4)
-    g_source, g_target, g_rel = gradients(1)
-    rel_sum[...] += g_rel
-    rel_all[rel] = rel_sum[...]
-    shares = []
-    for k in range(1, rels):
-        shares.append(
-            pltpu.make_async_remote_copy(
-                src_ref=rel_sum,
-                dst_ref=rel_all.at[rel],
-                send_sem=rsend_sem.at[k],
-                recv_sem=rrecv_sem.at[k],
-                device_id=(blk, lax.rem(rel + k, rels)),
-                device_id_type=MESH,
-            )
+    feed(5)
+    def share_with(peer, src_ref, dst_ref, k):
+        return pltpu.make_async_remote_copy(
+            src_ref=src_ref,
+            dst_ref=dst_ref,
+            send_sem=rsend_sem.at[k],
+            recv_sem=rrecv_sem.at[k],
+            device_id=(blk, peer),
+            device_id_type=MESH,
         )
-        shares[-1].start()
-
+
+    half = rels // 2
+    place = lax.rem(rel, half)
+    to_all = [
+        share_with(lax.rem(rel + k, rels), rel_sum, rel_all.at[rel], k) for k in range(1, rels)
+    ]
+    to_pair = share_with(lax.rem(rel + half, rels), rel_sum, rel_pair, 0)
+    to_side = [
+        share_with(
+            rel - place + lax.rem(place + k, half), rel_all.at[place], rel_all.at[place], k
+        )
+        for k in range(1, half)
+    ]
+
+    def exchange(g_rel):
+        rel_sum[...] += g_rel
+
+        @pl.when(core == 0)
+        def _():
+            for copy in to_all:
+                copy.start()
+            rel_all[rel] = rel_sum[...]
+
+        @pl.when(core == 1)
+        def _():
+            to_pair.start()
+            for k in range(half, rels):
+                rel_all[k] = jnp.zeros((NREL, D), f32)
+
+    g_source, g_target = gradients(1, exchange)
     high, low = halves(g_target)
     for c in range(CHUNKS):
-        update(c, high, low, hot_dst, grad_r, main1, state1)
+        update(c, high, low, hot_dst, grad_r[:, cut(c)], main1, state1)
+
+    @pl.when(core == 1)
+    def _():
+        to_pair.wait_recv()
+        rel_all[place] = rel_sum[...] + rel_pair[...]
+        for copy in to_side:
+            copy.start()
+
 
     high, low = halves(g_source)
     for c in range(CHUNKS):
-        update(c, high, low, hot_src, grad_l, left_m, left_s)
+        update(c, high, low, hot_src, left_grad(c), left_m, left_s)
 
     for move in moves[0] + moves[1][CHUNKS - FLIGHT :]:
         move.wait_send()
@@ -272,12 +331,20 @@
         for move in moves[1][: CHUNKS - FLIGHT]:
             move.wait_send()
 
-    for copy in shares:
-        copy.wait()
+    @pl.when(core == 0)
+    def _():
+        for copy in to_all:
+            copy.wait()
+
+    @pl.when(core == 1)
+    def _():
+        to_pair.wait_send()
+        for copy in to_side:
+            copy.wait()
 
 
 def put_out(
-    left, right, rel_all, rel_old, rel_state, left_out, right_out, relations_out, sem
+    left, right, rel_all, rel_old, rel_state, left_out, right_out, relations_out, rel_new, sem
 ):
     puts = []
     for c in range(PIECES):
@@ -290,7 +357,9 @@
     for k in range(1, rel_all.shape[0]):
         total = total + rel_all[k]
     state = rel_state[:, 0:1] + jnp.sum(total * total, axis=1, keepdims=True) / D
-    relations_out[0, :, :] = rel_old[...] - rate * total / jnp.sqrt(state)
+    rel_new[0, :, :] = rel_old[...] - rate * total / jnp.sqrt(state)
+    puts.append(pltpu.make_async_copy(rel_new, relations_out, sem.at[2 * PIECES]))
+    puts[-1].start()
     for put in puts:
         put.wait()
 
@@ -339,9 +408,15 @@
             pltpu.VMEM((NREL, D), f32),
             pltpu.VMEM((NREL, 128), f32),
         ),
-        in_specs=[hbm, vmem, hbm] + [vmem] * 8,
+        in_specs=[hbm] * 11,
         out_specs=(vmem,) * 5,
         scratch_shapes=[
+            pltpu.VMEM((1, NREL), f32),
+            pltpu.VMEM((2, EDGES), jnp.int32),
+            pltpu.VMEM((2, EDGES), jnp.int32),
+            pltpu.VMEM((2, EDGES), jnp.int32),
+            pltpu.VMEM((2, NEG), jnp.int32),
+            pltpu.VMEM((2, NEG), jnp.int32),
             rounded,
             row,
             rounded,
@@ -362,10 +437,11 @@
             pltpu.VMEM((D, EDGES), bf16),
             edge,
             edge,
-            slab,
+            pltpu.VMEM((EDGES, ROWS), bf16),
             slab,
             pltpu.VMEM((NREL, D), f32),
-            pltpu.SemaphoreType.DMA((1,)),
+            pltpu.VMEM((NREL, D), f32),
+            pltpu.SemaphoreType.DMA((9,)),
             pltpu.SemaphoreType.DMA((2, CHUNKS + 1)),
             pltpu.SemaphoreType.DMA((2, CHUNKS + 1)),
             pltpu.SemaphoreType.DMA((rels,)),
@@ -384,8 +460,11 @@
             jax.ShapeDtypeStruct((1, NREL, D), f32),
         ),
         in_specs=[vmem, vmem, vmem, vmem, vmem],
-        out_specs=(hbm, hbm, vmem),
-        scratch_shapes=[pltpu.SemaphoreType.DMA((2 * PIECES,))],
+        out_specs=(hbm, hbm, hbm),
+        scratch_shapes=[
+            pltpu.VMEM((1, NREL, D), f32),
+            pltpu.SemaphoreType.DMA((2 * PIECES + 1,)),
+        ],
         compiler_params=pltpu.CompilerParams(vmem_limit_bytes=4 * 2**20),
         name="put_out",
     )(*[pin(x, pltpu.VMEM) for x in held])

time: 99.4 us -> 95.8 us (0.964)
  Pallas kernels: 98.4 us -> 94.9 us
    pallas_call x1, Pallas kernels: 95 us -> 92 us  [local(): pl.pallas_call(kernel, out_shape=(pltpu.VMEM((D, ROWS), f32), pltpu.VMEM(...]
where the time goes in v1:
time: 95.8 us; the launch traced here: 95.7 us
  Pallas kernels  94.9 us (99%)
    pallas_call x1, Pallas kernels, local(): pl.pallas_call(kernel, out_shape=(pltpu.VMEM((D, ROWS), f32), pltpu.VMEM(...  92 us
    pallas_call x1, Pallas kernels, local(): pl.pallas_call(put_out, out_shape=(jax.ShapeDtypeStruct((D, ROWS), f32),...  2.83 us

profile of v1, /device:TPU:26, one launch (start us, length us, event | category | flops | bytes accessed | tf_op | source)
XLA Modules:
  0.0 95.7 jit_solution(11182306035838866748)
XLA Ops:
  0.6 92.0 %train.1 = (f32[400,2048]{1,0:T(8,128)S(1)}, f32[400,2048]{1,0:T(8,128)S(1)}, f32[8,32,400]{2,1,0:T(8,128)S(1)}, f32[32,400]{1,0:T(8,128)S(1)}, f32[32,128]{1,0:T(8,128)S(1)}) custom-call(f32[400,2048]{1,0:T(8,128)} %bitcast.7, f32[1,2048]{1,0:T(1,128)} %bitcast.9, f32[400,2048]{1,0:T(8,128)} %bitcast.8, f32[1,2048]{1,0:T(1,128)} %bitcast.10, ...), custom_call_target="tpu_custom_call" | custom-call | tf_op jit(solution)/shard_map/train/pallas_call | solution.py:402
  92.7 2.8 %put_out.1 = (f32[400,2048]{1,0:T(8,128)}, f32[400,2048]{1,0:T(8,128)}, f32[1,32,400]{2,1,0:T(8,128)}) custom-call(f32[400,2048]{1,0:T(8,128)S(1)} %get-tuple-element.11.left, f32[400,2048]{1,0:T(8,128)S(1)} %get-tuple-element.12.right, f32[8,32,400]{2,1,0:T(8,128)S(1)} %get-tuple-element.13.rel_all, f32[32,400]{1,0:T(8,128)S(1)} %get-tuple-element.14.rel_old, ...), custom_call_target="tpu_custom_call" | custom-call | tf_op jit(solution)/shard_map/put_out/pallas_call | solution.py:455

commit v2 on v1

--- a/solution.py
+++ b/solution.py
@@ -12,10 +12,12 @@
 NEG = 1000
 NREL = 32
 CHUNK = 256
-CHUNKS = ROWS // CHUNK
+SPANS = [(k, k + CHUNK) for k in range(0, ROWS - CHUNK, CHUNK)]
+SPANS += [(ROWS - CHUNK, ROWS - CHUNK // 2), (ROWS - CHUNK // 2, ROWS)]
+CHUNKS = len(SPANS)
 PIECES = 2
 FLIGHT = 3
-LATER = {2: 6, 7: 7}
+LATER = {2: 6, 5: 7, 7: 8}
 MESH = pl.DeviceIdType.MESH
 f32 = jnp.float32
 bf16 = jnp.bfloat16
@@ -37,11 +39,12 @@
 
 
 def cut(c):
-    return slice(c * CHUNK, (c + 1) * CHUNK)
+    return slice(*SPANS[c])
 
 
 def hot_chunk(index_row, c):
-    return jnp.where(iota((CHUNK, EDGES), 0) + c * CHUNK == index_row, 1.0, 0.0).astype(bf16)
+    start, stop = SPANS[c]
+    return jnp.where(iota((stop - start, EDGES), 0) + start == index_row, 1.0, 0.0).astype(bf16)
 
 
 def count_rows(index_row):
@@ -117,6 +120,27 @@
     for k in range(1, rels):
         peer = (blk, lax.rem(rel + k, rels))
         pl.semaphore_signal(barrier, inc=1, device_id=peer, device_id_type=MESH)
+    pl.semaphore_wait(barrier, rels)
+
+    def send(src_ref, dst_ref, t, i):
+        return pltpu.make_async_remote_copy(
+            src_ref=src_ref,
+            dst_ref=dst_ref,
+            send_sem=send_sem.at[t, i],
+            recv_sem=recv_sem.at[t, i],
+            device_id=after,
+            device_id_type=MESH,
+        )
+
+    mains, states = (main0, main1), (state0, state1)
+    moves = (
+        [send(right.at[:, cut(c)], main0.at[:, cut(c)], 0, c) for c in range(CHUNKS)]
+        + [send(rstate, state0, 0, CHUNKS)],
+        [send(main0.at[:, cut(c)], main1.at[:, cut(c)], 1, c) for c in range(CHUNKS)]
+        + [send(state0, state1, 1, CHUNKS)],
+    )
+    for move in moves[0]:
+        move.start()
     pairs = (
         (src_in, src),
         (dst_in, dst),
@@ -131,27 +155,6 @@
     gets = [pltpu.make_async_copy(a, b, local_sem.at[i]) for i, (a, b) in enumerate(pairs)]
     for get in gets:
         get.start()
-    pl.semaphore_wait(barrier, rels)
-
-    def send(src_ref, dst_ref, t, i):
-        return pltpu.make_async_remote_copy(
-            src_ref=src_ref,
-            dst_ref=dst_ref,
-            send_sem=send_sem.at[t, i],
-            recv_sem=recv_sem.at[t, i],
-            device_id=after,
-            device_id_type=MESH,
-        )
-
-    mains, states = (main0, main1), (state0, state1)
-    moves = (
-        [send(right.at[:, cut(c)], main0.at[:, cut(c)], 0, c) for c in range(CHUNKS)]
-        + [send(rstate, state0, 0, CHUNKS)],
-        [send(main0.at[:, cut(c)], main1.at[:, cut(c)], 1, c) for c in range(CHUNKS)]
-        + [send(state0, state1, 1, CHUNKS)],
-    )
-    for move in moves[0]:
-        move.start()
 
     for get in gets:
         get.wait()
@@ -187,7 +190,11 @@
         out[...] += dot(high, table, 1, 0) + (dot(middle, table, 1, 0) + dot(low, table, 1, 0))
 
     def times(often, c):
-        return jnp.concatenate([often[2 * c : 2 * c + 1, :], often[2 * c + 1 : 2 * c + 2, :]], axis=1)
+        return times_of(often, *SPANS[c])
+
+    def times_of(often, start, stop):
+        pieces = [often[k : k + 1, :] for k in range(start // 128, stop // 128)]
+        return pieces[0] if len(pieces) == 1 else jnp.concatenate(pieces, axis=1)
 
     def slope(mine, rows):
         half_score = dot(mine[...], rows, 1, 0)
@@ -216,12 +223,12 @@
         p = weight[...] * target[...]
         probe_t[...] = p.astype(bf16)
         probe[...] = p.T.astype(bf16) * 0.5
-        for c in range(0, CHUNKS, 2):
-            both = slice(c * CHUNK, (c + 2) * CHUNK)
+        for start in range(0, ROWS, 2 * CHUNK):
+            both = slice(start, start + 2 * CHUNK)
             rows = left_b[:, both]
             g = slope(probe, rows)
             g_left[:, both] = g
-            often = jnp.concatenate([times(often_l, c), times(often_l, c + 1)], axis=1)
+            often = times_of(often_l, start, start + 2 * CHUNK)
             gp[...] += dot(rows, (g.astype(f32) * often).astype(bf16), 1, 1)
         s, w, y = source[...], weight[...], target[...]
         pos = jnp.sum(s * w * y, axis=0, keepdims=True)
@@ -280,8 +287,17 @@
 
     half = rels // 2
     place = lax.rem(rel, half)
+    side = lax.div(rel, half)
     to_all = [
-        share_with(lax.rem(rel + k, rels), rel_sum, rel_all.at[rel], k) for k in range(1, rels)
+        share_with(
+            half * lax.rem(side + dx, 2) + lax.rem(place + dy, half),
+            rel_sum,
+            rel_all.at[rel],
+            half * dx + dy,
+        )
+        for dx in (1, 0)
+        for dy in (2, 1, 3, 0)
+        if dx or dy
     ]
     to_pair = share_with(lax.rem(rel + half, rels), rel_sum, rel_pair, 0)
     to_side = [
@@ -302,7 +318,6 @@
 
         @pl.when(core == 1)
         def _():
-            to_pair.start()
             for k in range(half, rels):
                 rel_all[k] = jnp.zeros((NREL, D), f32)
 
@@ -310,34 +325,30 @@
     high, low = halves(g_target)
     for c in range(CHUNKS):
         update(c, high, low, hot_dst, grad_r[:, cut(c)], main1, state1)
+    high, low = halves(g_source)
+    for c in range(CHUNKS):
+        update(c, high, low, hot_src, left_grad(c), left_m, left_s)
+
+    for move in moves[0] + moves[1][CHUNKS - FLIGHT :]:
+        move.wait_send()
+
+    @pl.when(core == 0)
+    def _():
+        for move in moves[1][: CHUNKS - FLIGHT]:
+            move.wait_send()
+
+    @pl.when(core == 0)
+    def _():
+        for copy in to_all:
+            copy.wait()
 
     @pl.when(core == 1)
     def _():
+        to_pair.start()
         to_pair.wait_recv()
         rel_all[place] = rel_sum[...] + rel_pair[...]
         for copy in to_side:
             copy.start()
-
-
-    high, low = halves(g_source)
-    for c in range(CHUNKS):
-        update(c, high, low, hot_src, left_grad(c), left_m, left_s)
-
-    for move in moves[0] + moves[1][CHUNKS - FLIGHT :]:
-        move.wait_send()
-
-    @pl.when(core == 0)
-    def _():
-        for move in moves[1][: CHUNKS - FLIGHT]:
-            move.wait_send()
-
-    @pl.when(core == 0)
-    def _():
-        for copy in to_all:
-            copy.wait()
-
-    @pl.when(core == 1)
-    def _():
         to_pair.wait_send()
         for copy in to_side:
             copy.wait()

time: 95.8 us -> 95.4 us (level); the launches traced: 95.7 us -> 94.3 us
  Pallas kernels: 94.9 us -> 93.5 us
    pallas_call x1, Pallas kernels: 92 us -> 90.6 us  [local(): pl.pallas_call(kernel, out_shape=(pltpu.VMEM((D, ROWS), f32), pltpu.VMEM(...]
where the time goes in v2:
time: 95.4 us; the launch traced here: 94.3 us
  Pallas kernels  93.5 us (98%)
    pallas_call x1, Pallas kernels, local(): pl.pallas_call(kernel, out_shape=(pltpu.VMEM((D, ROWS), f32), pltpu.VMEM(...  90.6 us
    pallas_call x1, Pallas kernels, local(): pl.pallas_call(put_out, out_shape=(jax.ShapeDtypeStruct((D, ROWS), f32),...  2.83 us

profile of v2, /device:TPU:26, one launch (start us, length us, event | category | flops | bytes accessed | tf_op | source)
XLA Modules:
  0.0 94.3 jit_solution(14197764290918366868)
XLA Ops:
  0.6 90.6 %train.1 = (f32[400,2048]{1,0:T(8,128)S(1)}, f32[400,2048]{1,0:T(8,128)S(1)}, f32[8,32,400]{2,1,0:T(8,128)S(1)}, f32[32,400]{1,0:T(8,128)S(1)}, f32[32,128]{1,0:T(8,128)S(1)}) custom-call(f32[400,2048]{1,0:T(8,128)} %bitcast.7, f32[1,2048]{1,0:T(1,128)} %bitcast.9, f32[400,2048]{1,0:T(8,128)} %bitcast.8, f32[1,2048]{1,0:T(1,128)} %bitcast.10, ...), custom_call_target="tpu_custom_call" | custom-call | tf_op jit(solution)/shard_map/train/pallas_call | solution.py:413
  91.3 2.8 %put_out.1 = (f32[400,2048]{1,0:T(8,128)}, f32[400,2048]{1,0:T(8,128)}, f32[1,32,400]{2,1,0:T(8,128)}) custom-call(f32[400,2048]{1,0:T(8,128)S(1)} %get-tuple-element.11.left, f32[400,2048]{1,0:T(8,128)S(1)} %get-tuple-element.12.right, f32[8,32,400]{2,1,0:T(8,128)S(1)} %get-tuple-element.13.rel_all, f32[32,400]{1,0:T(8,128)S(1)} %get-tuple-element.14.rel_old, ...), custom_call_target="tpu_custom_call" | custom-call | tf_op jit(solution)/shard_map/put_out/pallas_call | solution.py:466
